TPU v7x, 32 devices: a whole 2x2x4 slice. The times are simulated.
32 devices in a mesh: section: 8 (over y, x, core), expert: 4 (over z).
Axes of the slice: x: 2, y: 2, z: 4, core: 2. Of those that a mesh axis runs over, the one named last changes fastest.
Arguments:
- act_rows: bfloat16 [8, 512, 2048], P('section', 'expert'), may hold values from -6 to 6
- cot_rows: bfloat16 [8, 512, 2048], P('section', 'expert'), may hold values from -2.390625 to 2.390625
- expert_ids: int32 [8, 512, 1], P('section', 'expert'), may hold values from 0 to 3; in each aligned block of 128 rows (0 to 127, 128 to 255, ..., all dimensions but the last counted through in order) at most 64 rows name the same one
- w_gate: bfloat16 [8, 4, 2048, 128], P('section', 'expert'), may hold values from -0.125 to 0.125
- w_up: bfloat16 [8, 4, 2048, 128], P('section', 'expert'), may hold values from -0.125 to 0.125
- w_down: bfloat16 [8, 4, 128, 2048], P('section', 'expert'), may hold values from -0.375 to 0.375
Outputs:
- act_grad: bfloat16 [8, 512, 2048], P('section', 'expert')
- gate_grad: bfloat16 [8, 4, 2048, 128], P('section', 'expert')
- up_grad: bfloat16 [8, 4, 2048, 128], P('section', 'expert')
- down_grad: bfloat16 [8, 4, 128, 2048], P('section', 'expert')
Inputs may be any that keep to these rules, and one draw needn't show every extreme that they name: `expert_ids`: within the 128 rows of one device no expert is named by more than 64 rows, a bound that some block reaches; every expert serves rows somewhere.
All inputs are finite; a program needn't handle non-finite values.
Results may differ from a plain program's by a relative error of at most 0.0049.
Values may be sent and summed in bfloat16 or wider, within the bound.
A program may use at most 64 MiB of HBM per device.

v0:
```python
import jax
import jax.numpy as jnp
from jax import lax
from jax.sharding import PartitionSpec as P


def passed_along(value, axis, by):
    peers = lax.axis_size(axis)
    return lax.ppermute(value, axis, [(i, (i + by) % peers) for i in range(peers)])


def joined_halves(own_part, other_part, is_upper, axis_num):
    first_half = jnp.where(is_upper, other_part, own_part)
    second_half = jnp.where(is_upper, own_part, other_part)
    return jnp.concatenate([first_half, second_half], axis=axis_num)


def slot_work(flat_rows, width, gate_full, up_full, down_full):
    act_buf = flat_rows[:, :width]
    cot_buf = flat_rows[:, width:]
    gate_pre = jnp.dot(act_buf, gate_full, preferred_element_type=jnp.float32)
    up_pre = jnp.dot(act_buf, up_full, preferred_element_type=jnp.float32)
    sigma = jax.nn.sigmoid(gate_pre)
    activ = gate_pre * sigma
    hidden = (activ * up_pre).astype(jnp.bfloat16)
    hidden_grad = lax.dot_general(
        cot_buf, down_full, (((1,), (1,)), ((), ())), preferred_element_type=jnp.float32
    )
    gate_delta = (hidden_grad * up_pre * sigma * (1.0 + gate_pre * (1.0 - sigma))).astype(
        jnp.bfloat16
    )
    up_delta = (hidden_grad * activ).astype(jnp.bfloat16)
    back_wide = lax.dot_general(
        gate_delta, gate_full, (((1,), (1,)), ((), ())), preferred_element_type=jnp.float32
    ) + lax.dot_general(
        up_delta, up_full, (((1,), (1,)), ((), ())), preferred_element_type=jnp.float32
    )
    return (back_wide, hidden, gate_delta, up_delta)


def row_work(flat_rows, width, weights):
    back_wide, hidden, gate_delta, up_delta = slot_work(
        flat_rows, width, weights[0], weights[1], weights[2]
    )
    return (back_wide.astype(jnp.bfloat16), flat_rows, hidden, gate_delta, up_delta, 1)


def per_device(act_rows, cot_rows, expert_ids, w_gate, w_up, w_down):
    n_experts = lax.axis_size("expert")
    half_count = lax.axis_size("section") // 2
    row_count = act_rows.shape[1]
    width = act_rows.shape[2]
    half_units = w_gate.shape[3]
    capacity = 2 * row_count // n_experts
    is_upper = lax.axis_index("section") >= half_count
    own_weights = (w_gate[0, 0], w_up[0, 0], w_down[0, 0])
    other_weights = passed_along(
        (own_weights[0], own_weights[1], own_weights[2]), "section", half_count
    )
    weights = (
        joined_halves(own_weights[0], other_weights[0], is_upper, 1),
        joined_halves(own_weights[1], other_weights[1], is_upper, 1),
        joined_halves(own_weights[2], other_weights[2], is_upper, 0),
    )
    route_ids = expert_ids[0, :, 0]
    onehot = (route_ids[:, None] == jnp.arange(n_experts, dtype=jnp.int32)[None, :]).astype(
        jnp.int32
    )
    ranks = jnp.cumsum(onehot, axis=0) - onehot
    slots = jnp.sum(ranks * onehot, axis=1)
    places = route_ids * capacity + slots
    packed = jnp.concatenate([act_rows[0], cot_rows[0]], axis=1)
    send_buf = jnp.zeros((n_experts * capacity, 2 * width), jnp.bfloat16).at[places].set(packed)
    send_buf = send_buf.reshape(n_experts, capacity, 2 * width)
    received = lax.all_to_all(send_buf, "expert", split_axis=0, concat_axis=0, tiled=True)
    act_back, used_rows, hidden, gate_delta, up_delta, copies = row_work(
        received.reshape(-1, 2 * width), width, weights
    )
    returned = lax.all_to_all(
        act_back.reshape(n_experts, capacity, width),
        "expert",
        split_axis=0,
        concat_axis=0,
        tiled=True,
    )
    act_grad = returned.reshape(-1, width)[places]
    act_buf = used_rows[:, :width]
    cot_buf = used_rows[:, width:]
    contract = (((0,), (0,)), ((), ()))
    gate_part = lax.dot_general(act_buf, gate_delta, contract, preferred_element_type=jnp.float32)
    up_part = lax.dot_general(act_buf, up_delta, contract, preferred_element_type=jnp.float32)
    down_part = lax.dot_general(hidden, cot_buf, contract, preferred_element_type=jnp.float32)
    own_start = is_upper.astype(jnp.int32) * half_units
    other_start = half_units - own_start
    outgoing = (
        lax.dynamic_slice_in_dim(gate_part, other_start, half_units, 1),
        lax.dynamic_slice_in_dim(up_part, other_start, half_units, 1),
        lax.dynamic_slice_in_dim(down_part, other_start, half_units, 0),
    )
    incoming = passed_along((outgoing[0], outgoing[1], outgoing[2]), "section", half_count)
    gate_total = lax.dynamic_slice_in_dim(gate_part, own_start, half_units, 1) + incoming[0]
    up_total = lax.dynamic_slice_in_dim(up_part, own_start, half_units, 1) + incoming[1]
    down_total = lax.dynamic_slice_in_dim(down_part, own_start, half_units, 0) + incoming[2]
    return (
        act_grad[None],
        gate_total.astype(jnp.bfloat16)[None, None],
        up_total.astype(jnp.bfloat16)[None, None],
        down_total.astype(jnp.bfloat16)[None, None],
    )


def solution(mesh):
    placed = (
        P("section", "expert", None),
        P("section", "expert", None),
        P("section", "expert", None),
        P("section", "expert", None, None),
        P("section", "expert", None, None),
        P("section", "expert", None, None),
    )
    return jax.shard_map(
        per_device,
        mesh=mesh,
        in_specs=placed,
        out_specs=(
            P("section", "expert", None),
            P("section", "expert", None, None),
            P("section", "expert", None, None),
            P("section", "expert", None, None),
        ),
        check_vma=False,
    )
```

profile of v0, /device:TPU:0, one launch (start us, length us, event | category | flops | bytes accessed | tf_op | source)
XLA Modules:
  0.0 141.4 jit_solution(5080239756411456441)
XLA Ops:
  0.6 0.7 fusion.26
  1.5 0.8 select_reduce_fusion
  2.4 0.7 fusion.28
  3.0 4.3 %scatter_custom_fusion = bf16[256,4096]{1,0:T(8,128)(2,1)} fusion(s32[128]{0:T(128)S(1)} %fusion.28, bf16[128,2048]{1,0:T(8,128)(2,1)} %bitcast.46, bf16[]{:T(256)} %constant.36, bf16[128,2048]{1,0:T(8,128)(2,1)} %bitcast.47, bf16[]{:T(256)} %constant.10.clone.1), kind=kCustom, calls=%fused_computation.4 | custom fusion | flops 2097152 | bytes 3145732 | tf_op jit(solution)/shard_map/scatter | solution.py:73
  7.3 6.4 %all-to-all-start = ((bf16[4,64,4096]{2,1,0:T(8,128)(2,1)}), bf16[4,64,4096]{2,1,0:T(8,128)(2,1)S(1)}, u32[]{:S(2)}, u32[]{:S(2)}) async-start(bf16[4,64,4096]{2,1,0:T(8,128)(2,1)} %bitcast.42), calls=%async_computation | async-start | bytes 4194304 | tf_op jit(solution)/shard_map/all_to_all | solution.py:75
  13.8 1.5 %collective-permute-start.2 = (bf16[2048,128]{1,0:T(8,128)(2,1)S(1)}, bf16[2048,128]{1,0:T(8,128)(2,1)}, u32[]{:S(2)}, u32[]{:S(2)}) collective-permute-start(bf16[2048,128]{1,0:T(8,128)(2,1)S(1)} %bitcast.44), channel_id=1, source_target_pairs={{0,16},{4,20},{8,24},{12,28},{16,0},{20,4},{24,8},{28,12},{1,17},{... | collective-permute-start | bytes 1572872 | tf_op jit(solution)/shard_map/ppermute | solution.py:9
  15.8 1.5 %collective-permute-start = (bf16[128,2048]{1,0:T(8,128)(2,1)}, bf16[128,2048]{1,0:T(8,128)(2,1)}, u32[]{:S(2)}, u32[]{:S(2)}) collective-permute-start(bf16[128,2048]{1,0:T(8,128)(2,1)} %bitcast.8), channel_id=1, source_target_pairs={{0,16},{4,20},{8,24},{12,28},{16,0},{20,4},{24,8},{28,12},{1,17},{... | collective-permute-start | bytes 1572872 | tf_op jit(solution)/shard_map/ppermute | solution.py:9
  17.3 11.4 %collective-permute-done.2 = bf16[2048,128]{1,0:T(8,128)(2,1)} collective-permute-done((bf16[2048,128]{1,0:T(8,128)(2,1)S(1)}, bf16[2048,128]{1,0:T(8,128)(2,1)}, u32[]{:S(2)}, u32[]{:S(2)}) %collective-permute-start.2) | collective-permute-done | bytes 524320 | tf_op jit(solution)/shard_map/ppermute | solution.py:9
  28.8 1.3 broadcast_select_fusion.1
  30.0 10.0 %collective-permute-done.1 = bf16[2048,128]{1,0:T(8,128)(2,1)} collective-permute-done((bf16[2048,128]{1,0:T(8,128)(2,1)}, bf16[2048,128]{1,0:T(8,128)(2,1)}, u32[]{:S(2)}, u32[]{:S(2)}) %collective-permute-start.1) | collective-permute-done | bytes 524320 | tf_op jit(solution)/shard_map/ppermute | solution.py:9
  40.0 2.2 %broadcast_select_fusion.3 = (bf16[2048,128]{1,0:T(8,128)(2,1)}, bf16[2048,128]{1,0:T(8,128)(2,1)}) fusion(bf16[2048,128]{1,0:T(8,128)(2,1)} %collective-permute-done.1, pred[]{:T(512)S(6)} %ge.3, bf16[1,1,2048,128]{3,2,1,0:T(8,128)(2,1)} %param.10), kind=kLoop, calls=%fused_computation.36 | loop fusion | flops 524288 | bytes 2097153 | tf_op jit(solution)/shard_map/jit(_where)/select_n | solution.py:13
  42.2 7.5 %collective-permute-done = bf16[128,2048]{1,0:T(8,128)(2,1)} collective-permute-done((bf16[128,2048]{1,0:T(8,128)(2,1)}, bf16[128,2048]{1,0:T(8,128)(2,1)}, u32[]{:S(2)}, u32[]{:S(2)}) %collective-permute-start) | collective-permute-done | bytes 524320 | tf_op jit(solution)/shard_map/ppermute | solution.py:9
  49.8 2.2 %broadcast_select_fusion.5 = (bf16[128,2048]{1,0:T(8,128)(2,1)}, bf16[128,2048]{1,0:T(8,128)(2,1)}) fusion(bf16[128,2048]{1,0:T(8,128)(2,1)} %collective-permute-done, pred[]{:T(512)S(6)} %ge.3, bf16[1,1,128,2048]{3,2,1,0:T(8,128)(2,1)} %param.11), kind=kLoop, calls=%fused_computation.38 | loop fusion | flops 524288 | bytes 2097153 | tf_op jit(solution)/shard_map/jit(_where)/select_n | solution.py:13
  52.0 10.0 %all-to-all-done = bf16[4,64,4096]{2,1,0:T(8,128)(2,1)S(1)} async-done(((bf16[4,64,4096]{2,1,0:T(8,128)(2,1)}), bf16[4,64,4096]{2,1,0:T(8,128)(2,1)S(1)}, u32[]{:S(2)}, u32[]{:S(2)}) %all-to-all-start) | async-done | bytes 2097184 | tf_op jit(solution)/shard_map/all_to_all | solution.py:75
  62.5 0.6 copy-done.3
  63.7 0.6 multiply_convert_fusion.2
  64.8 1.8 %fusion.16 = f32[2048,256]{1,0:T(8,128)} fusion(bf16[256,256]{1,0:T(8,128)(2,1)S(1)} %get-tuple-element.11, bf16[256,4096]{1,0:T(8,128)(2,1)S(1)} %bitcast.39), kind=kOutput, calls=%fused_computation.24 | convolution fusion | flops 268435456 | bytes 3276800 | tf_op jit(solution)/shard_map/dot_general | solution.py:91
  67.2 1.3 copy-done.1
  68.5 1.1 constant_dynamic-slice_fusion.1
  69.5 1.5 %collective-permute-start.3 = (f32[2048,128]{1,0:T(8,128)}, f32[2048,128]{1,0:T(8,128)}, u32[]{:S(2)}, u32[]{:S(2)}) collective-permute-start(f32[2048,128]{1,0:T(8,128)} %constant_dynamic-slice_fusion.1), channel_id=1, source_target_pairs={{0,16},{4,20},{8,24},{12,28},{16,0},{20,4},{24,8},{28,12},{1,17},{... | collective-permute-start | bytes 3145736 | tf_op jit(solution)/shard_map/ppermute | solution.py:9
  71.1 1.5 %fusion = bf16[256,2048]{1,0:T(8,128)(2,1)} fusion(f32[256,2048]{1,0:T(8,128)S(1)} %fusion.14, bf16[256,256]{1,0:T(8,128)(2,1)S(1)} %get-tuple-element.10, bf16[2048,128]{1,0:T(8,128)(2,1)S(1)} %get-tuple-element.7, bf16[2048,128]{1,0:T(8,128)(2,1)S(1)} %get-tuple-element.6), kind=kOutput, calls=%fused_computation.3 | convolution fusion | flops 271581184 | bytes 4325376 | tf_op jit(solution)/shard_map/dot_general | solution.py:33
  72.5 3.5 %all-to-all-start.1 = ((bf16[4,64,2048]{2,1,0:T(8,128)(2,1)}), bf16[4,64,2048]{2,1,0:T(8,128)(2,1)S(1)}, u32[]{:S(2)}, u32[]{:S(2)}) async-start(bf16[4,64,2048]{2,1,0:T(8,128)(2,1)} %bitcast.43), calls=%async_computation.1 | async-start | bytes 2097152 | tf_op jit(solution)/shard_map/all_to_all | solution.py:79
  76.1 1.3 constant_dynamic-slice_fusion
  77.4 0.6 collective-permute-start.4
  78.6 1.6 %collective-permute-start.5 = (f32[128,2048]{1,0:T(8,128)S(1)}, f32[128,2048]{1,0:T(8,128)S(1)}, u32[]{:S(2)}, u32[]{:S(2)}) collective-permute-start(f32[128,2048]{1,0:T(8,128)S(1)} %constant_dynamic-slice_fusion.2), channel_id=1, source_target_pairs={{0,16},{4,20},{8,24},{12,28},{16,0},{20,4},{24,8},{28,12},{1,17},{... | collective-permute-start | bytes 3145736 | tf_op jit(solution)/shard_map/ppermute | solution.py:9
  80.2 15.8 %collective-permute-done.3 = f32[2048,128]{1,0:T(8,128)} collective-permute-done((f32[2048,128]{1,0:T(8,128)}, f32[2048,128]{1,0:T(8,128)}, u32[]{:S(2)}, u32[]{:S(2)}) %collective-permute-start.3) | collective-permute-done | bytes 1048608 | tf_op jit(solution)/shard_map/ppermute | solution.py:9
  96.0 2.1 %fusion.22 = bf16[1,1,2048,128]{3,2,1,0:T(8,128)(2,1)} fusion(f32[2048,128]{1,0:T(8,128)} %collective-permute-done.3, f32[2048,256]{1,0:T(8,128)S(1)} %copy-done.2, s32[]{:T(128)S(6)} %mul.53), kind=kLoop, calls=%fused_computation.30 | loop fusion | flops 524288 | bytes 2621444 | tf_op jit(solution)/shard_map/broadcast_in_dim | solution.py:106
  98.1 20.2 %collective-permute-done.4 = f32[2048,128]{1,0:T(8,128)S(1)} collective-permute-done((f32[2048,128]{1,0:T(8,128)S(1)}, f32[2048,128]{1,0:T(8,128)S(1)}, u32[]{:S(2)}, u32[]{:S(2)}) %collective-permute-start.4) | collective-permute-done | bytes 1048608 | tf_op jit(solution)/shard_map/ppermute | solution.py:9
  118.3 0.9 fusion.23
  119.2 19.6 %collective-permute-done.5 = f32[128,2048]{1,0:T(8,128)S(1)} collective-permute-done((f32[128,2048]{1,0:T(8,128)S(1)}, f32[128,2048]{1,0:T(8,128)S(1)}, u32[]{:S(2)}, u32[]{:S(2)}) %collective-permute-start.5) | collective-permute-done | bytes 1048608 | tf_op jit(solution)/shard_map/ppermute | solution.py:9
  138.8 0.9 fusion.24
  139.7 1.7 %gather_fusion = bf16[128,2048]{1,0:T(8,128)(2,1)} fusion(bf16[256,2048]{1,0:T(8,128)(2,1)S(1)} %bitcast.35, s32[1024]{0:T(1024)S(1)} %pad_clamp_fusion), kind=kCustom, calls=%fused_computation | custom fusion | bytes 1049088 | tf_op jit(solution)/shard_map/gather | solution.py:86
  (28 shorter events, 3.4 us)
Async XLA Ops:
  7.3 6.5 %copy-start.5 = (bf16[1,1,2048,128]{3,2,1,0:T(8,128)(2,1)S(1)}, bf16[1,1,2048,128]{3,2,1,0:T(8,128)(2,1)}, u32[]{:S(2)}) copy-start(bf16[1,1,2048,128]{3,2,1,0:T(8,128)(2,1)} %param.9) | copy-start | bytes 1572868
  7.3 54.6 %all-to-all-start = ((bf16[4,64,4096]{2,1,0:T(8,128)(2,1)}), bf16[4,64,4096]{2,1,0:T(8,128)(2,1)S(1)}, u32[]{:S(2)}, u32[]{:S(2)}) async-start(bf16[4,64,4096]{2,1,0:T(8,128)(2,1)} %bitcast.42), calls=%async_computation | async-start | bytes 4194304 | tf_op jit(solution)/shard_map/all_to_all | solution.py:75
  13.8 15.0 %collective-permute-start.2 = (bf16[2048,128]{1,0:T(8,128)(2,1)S(1)}, bf16[2048,128]{1,0:T(8,128)(2,1)}, u32[]{:S(2)}, u32[]{:S(2)}) collective-permute-start(bf16[2048,128]{1,0:T(8,128)(2,1)S(1)} %bitcast.44), channel_id=1, source_target_pairs={{0,16},{4,20},{8,24},{12,28},{16,0},{20,4},{24,8},{28,12},{1,17},{... | collective-permute-start | bytes 1572872 | tf_op jit(solution)/shard_map/ppermute | solution.py:9
  15.3 24.7 %collective-permute-start.1 = (bf16[2048,128]{1,0:T(8,128)(2,1)}, bf16[2048,128]{1,0:T(8,128)(2,1)}, u32[]{:S(2)}, u32[]{:S(2)}) collective-permute-start(bf16[2048,128]{1,0:T(8,128)(2,1)} %bitcast.9), channel_id=1, source_target_pairs={{0,16},{4,20},{8,24},{12,28},{16,0},{20,4},{24,8},{28,12},{1,17},{... | collective-permute-start | bytes 1572872 | tf_op jit(solution)/shard_map/ppermute | solution.py:9
  15.8 33.9 %collective-permute-start = (bf16[128,2048]{1,0:T(8,128)(2,1)}, bf16[128,2048]{1,0:T(8,128)(2,1)}, u32[]{:S(2)}, u32[]{:S(2)}) collective-permute-start(bf16[128,2048]{1,0:T(8,128)(2,1)} %bitcast.8), channel_id=1, source_target_pairs={{0,16},{4,20},{8,24},{12,28},{16,0},{20,4},{24,8},{28,12},{1,17},{... | collective-permute-start | bytes 1572872 | tf_op jit(solution)/shard_map/ppermute | solution.py:9
  62.0 1.0 copy-start.3
  62.0 1.2 copy-start.4
  62.4 1.2 copy-start.6
  62.5 1.3 copy-start.7
  63.7 0.7 copy-start.8
  67.1 1.3 copy-start.1
  69.5 26.4 %collective-permute-start.3 = (f32[2048,128]{1,0:T(8,128)}, f32[2048,128]{1,0:T(8,128)}, u32[]{:S(2)}, u32[]{:S(2)}) collective-permute-start(f32[2048,128]{1,0:T(8,128)} %constant_dynamic-slice_fusion.1), channel_id=1, source_target_pairs={{0,16},{4,20},{8,24},{12,28},{16,0},{20,4},{24,8},{28,12},{1,17},{... | collective-permute-start | bytes 3145736 | tf_op jit(solution)/shard_map/ppermute | solution.py:9
  72.5 67.2 %all-to-all-start.1 = ((bf16[4,64,2048]{2,1,0:T(8,128)(2,1)}), bf16[4,64,2048]{2,1,0:T(8,128)(2,1)S(1)}, u32[]{:S(2)}, u32[]{:S(2)}) async-start(bf16[4,64,2048]{2,1,0:T(8,128)(2,1)} %bitcast.43), calls=%async_computation.1 | async-start | bytes 2097152 | tf_op jit(solution)/shard_map/all_to_all | solution.py:79
  76.0 1.9 %copy-start.9 = (f32[256,256]{1,0:T(8,128)S(1)}, f32[256,256]{1,0:T(8,128)}, u32[]{:S(2)}) copy-start(f32[256,256]{1,0:T(8,128)} %copy-done.8) | copy-start | bytes 786436
  77.4 18.5 %copy-start.2 = (f32[2048,256]{1,0:T(8,128)S(1)}, f32[2048,256]{1,0:T(8,128)}, u32[]{:S(2)}) copy-start(f32[2048,256]{1,0:T(8,128)} %copy-done.1) | copy-start | bytes 6291460
  77.4 40.9 %collective-permute-start.4 = (f32[2048,128]{1,0:T(8,128)S(1)}, f32[2048,128]{1,0:T(8,128)S(1)}, u32[]{:S(2)}, u32[]{:S(2)}) collective-permute-start(f32[2048,128]{1,0:T(8,128)S(1)} %constant_dynamic-slice_fusion), channel_id=1, source_target_pairs={{0,16},{4,20},{8,24},{12,28},{16,0},{20,4},{24,8},{28,12},{1,17},{... | collective-permute-start | bytes 3145736 | tf_op jit(solution)/shard_map/ppermute | solution.py:9
  78.5 39.8 %copy-start = (f32[2048,256]{1,0:T(8,128)S(1)}, f32[2048,256]{1,0:T(8,128)}, u32[]{:S(2)}) copy-start(f32[2048,256]{1,0:T(8,128)} %fusion.16) | copy-start | bytes 6291460
  78.6 60.2 %collective-permute-start.5 = (f32[128,2048]{1,0:T(8,128)S(1)}, f32[128,2048]{1,0:T(8,128)S(1)}, u32[]{:S(2)}, u32[]{:S(2)}) collective-permute-start(f32[128,2048]{1,0:T(8,128)S(1)} %constant_dynamic-slice_fusion.2), channel_id=1, source_target_pairs={{0,16},{4,20},{8,24},{12,28},{16,0},{20,4},{24,8},{28,12},{1,17},{... | collective-permute-start | bytes 3145736 | tf_op jit(solution)/shard_map/ppermute | solution.py:9
where the time goes:
time: 142 us; the launch traced here: 141 us
  waiting for transfers between devices  94.5 us (67%)
  starting transfers between devices  17.2 us (12%)
  other arithmetic  16.4 us (12%)
  local copies, waits for them, and re-layouts  6.4 us (5%)
  matrix products  6.18 us (4%)
    ppermute x6, waiting for transfers between devices, passed_along(): lax.ppermute(value, axis, [(i, (i + by) % peers) for i in range(peers)])  84.5 us
    all_to_all x1, waiting for transfers between devices, per_device(): lax.all_to_all(send_buf, 'expert', split_axis=0, concat_axis=0, tiled=True)  10 us
    ppermute x6, starting transfers between devices, passed_along(): lax.ppermute(value, axis, [(i, (i + by) % peers) for i in range(peers)])  7.22 us
    all_to_all x1, starting transfers between devices, per_device(): lax.all_to_all(send_buf, 'expert', split_axis=0, concat_axis=0, tiled=True)  6.45 us
    select_n x3, other arithmetic, joined_halves(): first_half = jnp.where(is_upper, other_part, own_part)  5.75 us
    scatter x1, other arithmetic, per_device(): jnp.zeros((n_experts * capacity, 2 * width), jnp.bfloat16).at[places]  4.3 us
    all_to_all x1, starting transfers between devices, per_device(): lax.all_to_all(act_back.reshape(n_experts, capacity, width), 'expert', sp...  3.51 us
  transfers between devices with their start and end apart: 8, of which 7 were waited for; matrix products, arithmetic and copies ran while one was open for 9% of the time, Pallas kernels for 0%

commit v1 on v0

v1 whole, which is shorter than its diff:
```python
import functools
import math

import jax
import jax.numpy as jnp
from jax import lax
from jax.experimental import pallas as pl
from jax.experimental.pallas import tpu as pltpu
from jax.sharding import PartitionSpec as P

MESH = pl.DeviceIdType.MESH
F32 = jnp.float32
BF16 = jnp.bfloat16


def dot(a, b, a_dim, b_dim):
    return lax.dot_general(a, b, (((a_dim,), (b_dim,)), ((), ())), preferred_element_type=F32)


def partner_of(own, k, count):
    other = own
    bit = 1
    while bit < count:
        if k & bit:
            other = other + bit - 2 * bit * ((own // bit) % 2)
        bit *= 2
    return other


def kernel(
    n_experts, n_groups, cap,
    act_ref, cot_ref, ids_ref, wg_ref, wu_ref, wd_ref,
    out_ref, gate_ref, up_ref, down_ref,
    w_cat, send_a, send_c, rows_a, rows_c, delta, hidden, own_back, mate_out, mate_in, ret_out, ret_in,
    zs, zr, ys, yr, bs, br, rs, rr,
):
    n_rows, width = act_ref.shape
    units = wg_ref.shape[1]
    slots = n_experts * cap
    group = slots // n_groups
    per_group = n_experts // n_groups
    half = lax.axis_size("section") // 2
    section = lax.axis_index("section")
    own = lax.axis_index("expert")
    mate = {"section": (section + half) % (2 * half)}
    partners = [{"expert": partner_of(own, k, n_experts)} for k in range(n_experts)]

    barrier = pltpu.get_barrier_semaphore()
    for peer in partners[1:] + [mate]:
        pl.semaphore_signal(barrier, inc=1, device_id=peer, device_id_type=MESH)

    def remote(src, dst, send_sem, recv_sem, peer):
        return pltpu.make_async_remote_copy(
            src_ref=src, dst_ref=dst, send_sem=send_sem, recv_sem=recv_sem, device_id=peer, device_id_type=MESH
        )

    def chunk(k):
        return pl.ds(k * cap, cap)

    def rows_of(g, section_part=0):
        return pl.ds(section_part * slots + g * group, group)

    z_copies = [None] + [
        [
            remote(send_a.at[chunk(k)], rows_a.at[chunk(k)], zs.at[0, k], zr.at[0, k], partners[k]),
            remote(send_c.at[chunk(k)], rows_c.at[chunk(k)], zs.at[1, k], zr.at[1, k], partners[k]),
        ]
        for k in range(1, n_experts)
    ]
    y_copies = [
        [
            remote(rows_a.at[rows_of(g)], rows_a.at[rows_of(g, 1)], ys.at[0, g], yr.at[0, g], mate),
            remote(rows_c.at[rows_of(g)], rows_c.at[rows_of(g, 1)], ys.at[1, g], yr.at[1, g], mate),
        ]
        for g in range(n_groups)
    ]
    b_copies = [
        remote(mate_out.at[rows_of(g)], mate_in.at[rows_of(g)], bs.at[g], br.at[g], mate) for g in range(n_groups)
    ]
    r_copies = [None] + [
        remote(ret_out.at[chunk(k)], ret_in.at[chunk(k)], rs.at[k], rr.at[k], partners[k])
        for k in range(1, n_experts)
    ]

    rel = ids_ref[...] ^ own
    onehot = (lax.broadcasted_iota(jnp.int32, (n_rows, 128), 1) == rel).astype(F32)
    below = (
        lax.broadcasted_iota(jnp.int32, (n_rows, n_rows), 0) > lax.broadcasted_iota(jnp.int32, (n_rows, n_rows), 1)
    ).astype(F32)
    ranks = dot(below.astype(BF16), onehot.astype(BF16), 1, 0)
    place = rel * cap + jnp.sum(ranks * onehot, axis=1, keepdims=True).astype(jnp.int32)
    spread = (lax.broadcasted_iota(jnp.int32, (n_rows, slots), 1) == place).astype(F32).astype(BF16)

    packed = dot(spread, act_ref[...], 0, 0).astype(BF16)
    send_a[...] = packed
    rows_a[chunk(0)] = packed[:cap]
    packed = dot(spread, cot_ref[...], 0, 0).astype(BF16)
    send_c[...] = packed
    rows_c[chunk(0)] = packed[:cap]

    pl.semaphore_wait(barrier, n_experts)
    order = [0, 1, 3, 2] if n_groups == 4 else list(range(n_groups))
    for g in order:
        for k in range(g * per_group, (g + 1) * per_group):
            if k > 0:
                for copy in z_copies[k]:
                    copy.start()

    w_cat[:, :units] = wg_ref[...]
    w_cat[:, units:] = wu_ref[...]

    def arrive(g):
        for part in range(2):
            for k in range(g * per_group, (g + 1) * per_group):
                if k > 0:
                    z_copies[k][part].wait_recv()
            y_copies[g][part].start()

    def work(rows):
        pre = dot(rows_a[rows], w_cat[...], 1, 0)
        gate_pre, up_pre = pre[:, :units], pre[:, units:]
        hidden_grad = dot(rows_c[rows], wd_ref[...], 1, 1)
        sigma = 1.0 / (1.0 + jnp.exp(-gate_pre))
        activ = gate_pre * sigma
        hidden[rows] = (activ * up_pre).astype(BF16)
        delta[rows, :units] = (hidden_grad * up_pre * sigma * (1.0 + gate_pre * (1.0 - sigma))).astype(BF16)
        delta[rows, units:] = (hidden_grad * activ).astype(BF16)
        return dot(delta[rows], w_cat[...], 1, 1)

    def own_work(g):
        own_back[rows_of(g)] = work(rows_of(g))

    def mate_work(g):
        for copy in y_copies[g]:
            copy.wait_recv()
        mate_out[rows_of(g)] = work(rows_of(g, 1)).astype(BF16)
        b_copies[g].start()

    def give_back(g):
        b_copies[g].wait_recv()
        total = (own_back[rows_of(g)] + mate_in[rows_of(g)].astype(F32)).astype(BF16)
        ret_out[rows_of(g)] = total
        for k in range(g * per_group, (g + 1) * per_group):
            if k > 0:
                r_copies[k].start()
            else:
                ret_in[chunk(0)] = total[:cap]

    for i in range(n_groups + 2):
        if i < n_groups:
            arrive(order[i])
            own_work(order[i])
        if 1 <= i <= n_groups:
            mate_work(order[i - 1])
        if i >= 2:
            give_back(order[i - 2])

    tile = 256
    for at in range(0, width, tile):
        cols = pl.ds(at, tile)
        grads = dot(rows_a[:, cols], delta[...], 0, 0)
        gate_ref[cols] = grads[:, :units].astype(BF16)
        up_ref[cols] = grads[:, units:].astype(BF16)
    down_ref[...] = dot(hidden[...], rows_c[...], 0, 0).astype(BF16)

    for copy in r_copies[1:]:
        copy.wait_recv()
    out_ref[...] = dot(spread, ret_in[...], 1, 0).astype(BF16)

    for k in range(1, n_experts):
        for copy in z_copies[k]:
            copy.wait_send()
        r_copies[k].wait_send()
    for g in range(n_groups):
        for copy in y_copies[g]:
            copy.wait_send()
        b_copies[g].wait_send()


def per_device(act_rows, cot_rows, expert_ids, w_gate, w_up, w_down):
    n_experts = lax.axis_size("expert")
    n_rows, width = act_rows.shape[1:]
    units = w_gate.shape[3]
    cap = 2 * n_rows // n_experts
    slots = n_experts * cap
    n_groups = math.gcd(n_experts, 4)
    dma = pltpu.SemaphoreType.DMA
    vmem = pl.BlockSpec(memory_space=pltpu.VMEM)
    outs = pl.pallas_call(
        functools.partial(kernel, n_experts, n_groups, cap),
        out_shape=(
            jax.ShapeDtypeStruct((n_rows, width), BF16),
            jax.ShapeDtypeStruct((width, units), BF16),
            jax.ShapeDtypeStruct((width, units), BF16),
            jax.ShapeDtypeStruct((units, width), BF16),
        ),
        in_specs=[vmem] * 6,
        out_specs=(vmem,) * 4,
        scratch_shapes=[
            pltpu.VMEM((width, 2 * units), BF16),
            pltpu.VMEM((slots, width), BF16),
            pltpu.VMEM((slots, width), BF16),
            pltpu.VMEM((2 * slots, width), BF16),
            pltpu.VMEM((2 * slots, width), BF16),
            pltpu.VMEM((2 * slots, 2 * units), BF16),
            pltpu.VMEM((2 * slots, units), BF16),
            pltpu.VMEM((slots, width), F32),
            pltpu.VMEM((slots, width), BF16),
            pltpu.VMEM((slots, width), BF16),
            pltpu.VMEM((slots, width), BF16),
            pltpu.VMEM((slots, width), BF16),
            dma((2, n_experts)),
            dma((2, n_experts)),
            dma((2, n_groups)),
            dma((2, n_groups)),
            dma((n_groups,)),
            dma((n_groups,)),
            dma((n_experts,)),
            dma((n_experts,)),
        ],
        compiler_params=pltpu.CompilerParams(
            collective_id=0, has_side_effects=True, vmem_limit_bytes=48 * 1024 * 1024
        ),
        cost_estimate=pl.CostEstimate(
            flops=32 * slots * width * units, bytes_accessed=9 * n_rows * width * 2, transcendentals=2 * slots * units
        ),
    )(act_rows[0], cot_rows[0], expert_ids[0], w_gate[0, 0], w_up[0, 0], w_down[0, 0])
    return (outs[0][None], outs[1][None, None], outs[2][None, None], outs[3][None, None])


def solution(mesh):
    rows = P("section", "expert", None)
    weights = P("section", "expert", None, None)
    return jax.shard_map(
        per_device,
        mesh=mesh,
        in_specs=(rows, rows, rows, weights, weights, weights),
        out_specs=(rows, weights, weights, weights),
        check_vma=False,
    )
```

time: 142 us -> 101 us (0.71)
  waiting for transfers between devices: 94.5 us -> 0 us
  Pallas kernels: 0 us -> 91 us
  starting transfers between devices: 17.2 us -> 0 us
  other arithmetic: 16.4 us -> 0 us
  matrix products: 6.18 us -> 0 us
  local copies, waits for them, and re-layouts: 6.4 us -> 9.14 us
    pallas_call x0 -> x1, Pallas kernels: none -> 91 us  [per_device(): pl.pallas_call(functools.partial(kernel, n_experts, n_groups, cap), out_s...]
    ppermute x6 -> x0, waiting for transfers between devices: 84.5 us -> none  [passed_along(): lax.ppermute(value, axis, [(i, (i + by) % peers) for i in range(peers)])]
    all_to_all x2 -> x0, waiting for transfers between devices: 10 us -> none  [the longest x1 10 us: per_device(): lax.all_to_all(send_buf, 'expert', split_axis=0, concat_axis=0, tiled=True)]
    all_to_all x2 -> x0, starting transfers between devices: 9.96 us -> none  [the longest x1 6.45 us: per_device(): lax.all_to_all(send_buf, 'expert', split_axis=0, concat_axis=0, tiled=True)]
    ppermute x6 -> x0, starting transfers between devices: 7.22 us -> none  [passed_along(): lax.ppermute(value, axis, [(i, (i + by) % peers) for i in range(peers)])]
    unnamed x20 -> x16, local copies, waits for them, and re-layouts: 2.2 us -> 9.02 us
    select_n x4 -> x0, other arithmetic: 6.41 us -> none  [the longest x3 5.75 us: joined_halves(): first_half = jnp.where(is_upper, other_part, own_part)]
    dot_general x8 -> x0, matrix products: 6.18 us -> none  [the longest x1 1.82 us: per_device(): lax.dot_general(act_buf, up_delta, contract, preferred_element_type=jnp.f...]
  transfers between devices with their start and end apart: 8 -> 0, of which waited for: 7 -> 0; matrix products, arithmetic and copies ran while one was open for 9% -> 0% of each run, Pallas kernels for 0% -> 0%
where the time goes in v1:
time: 101 us
  Pallas kernels  91 us (90%)
  local copies, waits for them, and re-layouts  9.14 us (9%)
    pallas_call x1, Pallas kernels, per_device(): pl.pallas_call(functools.partial(kernel, n_experts, n_groups, cap), out_s...  91 us
    unnamed x16, local copies, waits for them, and re-layouts  9.02 us

profile of v1, /device:TPU:0, one launch (start us, length us, event | category | flops | bytes accessed | tf_op | source)
XLA Modules:
  0.0 100.8 jit_solution(11730517080641407217)
XLA Ops:
  0.6 0.0 copy-start.5
  0.6 0.6 copy-done.5
  1.3 0.1 copy.10.ids_ref
  1.4 0.0 copy-start
  1.4 1.0 %copy-done = bf16[1,128,2048]{2,1,0:T(8,128)(2,1)S(1)} copy-done((bf16[1,128,2048]{2,1,0:T(8,128)(2,1)S(1)}, bf16[1,128,2048]{2,1,0:T(8,128)(2,1)}, u32[]{:S(2)}) %copy-start) | copy-done | bytes 524312
  2.4 0.0 copy-start.1
  2.4 1.0 %copy-done.1 = bf16[1,128,2048]{2,1,0:T(8,128)(2,1)S(1)} copy-done((bf16[1,128,2048]{2,1,0:T(8,128)(2,1)S(1)}, bf16[1,128,2048]{2,1,0:T(8,128)(2,1)}, u32[]{:S(2)}) %copy-start.1) | copy-done | bytes 524312
  3.5 0.0 copy-start.2
  3.5 1.0 %copy-done.2 = bf16[1,1,2048,128]{3,2,1,0:T(8,128)(2,1)S(1)} copy-done((bf16[1,1,2048,128]{3,2,1,0:T(8,128)(2,1)S(1)}, bf16[1,1,2048,128]{3,2,1,0:T(8,128)(2,1)}, u32[]{:S(2)}) %copy-start.2) | copy-done | bytes 524312
  4.5 0.0 copy-start.3
  4.5 1.0 %copy-done.3 = bf16[1,1,2048,128]{3,2,1,0:T(8,128)(2,1)S(1)} copy-done((bf16[1,1,2048,128]{3,2,1,0:T(8,128)(2,1)S(1)}, bf16[1,1,2048,128]{3,2,1,0:T(8,128)(2,1)}, u32[]{:S(2)}) %copy-start.3) | copy-done | bytes 524312
  5.6 0.0 copy-start.4
  5.6 1.0 %copy-done.4 = bf16[1,1,128,2048]{3,2,1,0:T(8,128)(2,1)S(1)} copy-done((bf16[1,1,128,2048]{3,2,1,0:T(8,128)(2,1)S(1)}, bf16[1,1,128,2048]{3,2,1,0:T(8,128)(2,1)}, u32[]{:S(2)}) %copy-start.4) | copy-done | bytes 524312
  6.6 91.0 %shard_map.93 = (bf16[128,2048]{1,0:T(8,128)(2,1)S(1)}, bf16[2048,128]{1,0:T(8,128)(2,1)S(1)}, bf16[2048,128]{1,0:T(8,128)(2,1)S(1)}, bf16[128,2048]{1,0:T(8,128)(2,1)S(1)}) custom-call(bf16[128,2048]{1,0:T(8,128)(2,1)S(1)} %bitcast.14, bf16[128,2048]{1,0:T(8,128)(2,1)S(1)} %bitcast.15, s32[128,1]{1,0:T(8,128)S(1)} %copy.10.ids_ref, ...), custom_call_target="tpu_custom_call" | custom-call | flops 2147483648 | bytes 4718592 | tf_op jit(solution)/shard_map/pallas_call | solution.py:189
  97.6 0.8 copy.15
  98.4 0.8 copy.16
  99.2 0.8 copy.17
  100.0 0.8 copy.18
Async XLA Ops:
  0.6 0.7 copy-start.5
  1.4 1.0 %copy-start = (bf16[1,128,2048]{2,1,0:T(8,128)(2,1)S(1)}, bf16[1,128,2048]{2,1,0:T(8,128)(2,1)}, u32[]{:S(2)}) copy-start(bf16[1,128,2048]{2,1,0:T(8,128)(2,1)} %param.6) | copy-start | bytes 1572868
  2.4 1.0 %copy-start.1 = (bf16[1,128,2048]{2,1,0:T(8,128)(2,1)S(1)}, bf16[1,128,2048]{2,1,0:T(8,128)(2,1)}, u32[]{:S(2)}) copy-start(bf16[1,128,2048]{2,1,0:T(8,128)(2,1)} %param.7) | copy-start | bytes 1572868
  3.5 1.0 %copy-start.2 = (bf16[1,1,2048,128]{3,2,1,0:T(8,128)(2,1)S(1)}, bf16[1,1,2048,128]{3,2,1,0:T(8,128)(2,1)}, u32[]{:S(2)}) copy-start(bf16[1,1,2048,128]{3,2,1,0:T(8,128)(2,1)} %param.9) | copy-start | bytes 1572868
  4.5 1.0 %copy-start.3 = (bf16[1,1,2048,128]{3,2,1,0:T(8,128)(2,1)S(1)}, bf16[1,1,2048,128]{3,2,1,0:T(8,128)(2,1)}, u32[]{:S(2)}) copy-start(bf16[1,1,2048,128]{3,2,1,0:T(8,128)(2,1)} %param.10) | copy-start | bytes 1572868
  5.6 1.0 %copy-start.4 = (bf16[1,1,128,2048]{3,2,1,0:T(8,128)(2,1)S(1)}, bf16[1,1,128,2048]{3,2,1,0:T(8,128)(2,1)}, u32[]{:S(2)}) copy-start(bf16[1,1,128,2048]{3,2,1,0:T(8,128)(2,1)} %param.11) | copy-start | bytes 1572868

commit v2 on v1

v2 whole, which is shorter than its diff:
```python
import functools

import jax
import jax.numpy as jnp
from jax import lax
from jax.experimental import pallas as pl
from jax.experimental.pallas import tpu as pltpu
from jax.sharding import PartitionSpec as P

MESH = pl.DeviceIdType.MESH
F32 = jnp.float32
BF16 = jnp.bfloat16


def dot(a, b, a_dim, b_dim):
    return lax.dot_general(a, b, (((a_dim,), (b_dim,)), ((), ())), preferred_element_type=F32)


def partner_of(own, k, count):
    other = own
    bit = 1
    while bit < count:
        if k & bit:
            other = other + bit - 2 * bit * ((own // bit) % 2)
        bit *= 2
    return other


def kernel(
    n_experts, n_groups, cap,
    act_ref, cot_ref, ids_ref, wg_ref, wu_ref, wd_ref,
    out_hbm, gate_hbm, up_hbm, down_hbm,
    out_ref, gate_ref, up_ref, down_ref, act, cot, w_cat, wd, send, rows, delta, hidden, own_back, mate_out, mate_in, ret_out, ret_in,
    loads, stores, zs, zr, ys, yr, bs, br, rs, rr,
):
    n_rows, width = act_ref.shape
    units = wg_ref.shape[1]
    slots = n_experts * cap
    group = slots // n_groups
    piece = min(cap, group)
    n_pieces = slots // piece
    per_group = n_pieces // n_groups
    half = lax.axis_size("section") // 2
    section = lax.axis_index("section")
    own = lax.axis_index("expert")
    mate = {"section": (section + half) % (2 * half)}
    partners = [{"expert": partner_of(own, k, n_experts)} for k in range(n_experts)]

    fetch = [
        pltpu.make_async_copy(src, dst, loads.at[i])
        for i, (src, dst) in enumerate(
            [
                (act_ref, act),
                (cot_ref, cot),
                (wg_ref, w_cat.at[:, pl.ds(0, units)]),
                (wu_ref, w_cat.at[:, pl.ds(units, units)]),
                (wd_ref, wd),
            ]
        )
    ]
    for copy in fetch:
        copy.start()

    barrier = pltpu.get_barrier_semaphore()
    for peer in partners[1:] + [mate]:
        pl.semaphore_signal(barrier, inc=1, device_id=peer, device_id_type=MESH)

    def remote(src, dst, send_sem, recv_sem, peer):
        return pltpu.make_async_remote_copy(
            src_ref=src, dst_ref=dst, send_sem=send_sem, recv_sem=recv_sem, device_id=peer, device_id_type=MESH
        )

    def peer_of(p):
        return p * piece // cap

    def piece_rows(p):
        return pl.ds(p * piece, piece)

    def rows_of(g, section_part=0):
        return pl.ds(section_part * slots + g * group, group)

    def pieces(g):
        return [p for p in range(g * per_group, (g + 1) * per_group) if peer_of(p) > 0]

    z_copies = [
        remote(send.at[piece_rows(p)], rows.at[piece_rows(p)], zs.at[p], zr.at[p], partners[peer_of(p)])
        if peer_of(p) > 0 else None
        for p in range(n_pieces)
    ]
    y_copies = [remote(rows.at[rows_of(g)], rows.at[rows_of(g, 1)], ys.at[g], yr.at[g], mate) for g in range(n_groups)]
    b_copies = [
        remote(mate_out.at[rows_of(g)], mate_in.at[rows_of(g)], bs.at[g], br.at[g], mate) for g in range(n_groups)
    ]
    r_copies = [
        remote(ret_out.at[piece_rows(p)], ret_in.at[piece_rows(p)], rs.at[p], rr.at[p], partners[peer_of(p)])
        if peer_of(p) > 0 else None
        for p in range(n_pieces)
    ]

    rel = ids_ref[...] ^ own
    kinds = -(-n_experts // 16) * 16
    onehot = (lax.broadcasted_iota(jnp.int32, (kinds, n_rows), 0) == rel).astype(F32)
    above = (
        lax.broadcasted_iota(jnp.int32, (n_rows, n_rows), 0) < lax.broadcasted_iota(jnp.int32, (n_rows, n_rows), 1)
    ).astype(F32)
    ranks = dot(onehot.astype(BF16), above.astype(BF16), 1, 0)
    place = rel * cap + jnp.sum(ranks * onehot, axis=0, keepdims=True).astype(jnp.int32)
    spread = (lax.broadcasted_iota(jnp.int32, (slots, n_rows), 0) == place).astype(F32).astype(BF16)

    for i, source in enumerate((act, cot)):
        fetch[i].wait()
        packed = dot(spread, source[...], 1, 0).astype(BF16)
        cols = pl.ds(i * width, width)
        send[cap:, cols] = packed[cap:]
        rows[:cap, cols] = packed[:cap]

    order = list(range(n_groups))
    if n_groups == 8:
        order = [0, 1, 2, 3, 6, 7, 4, 5]
    late = order[-2:]

    def send_group(g):
        for p in pieces(g):
            z_copies[p].start()

    def sent_group(g):
        for p in pieces(g):
            z_copies[p].wait_send()

    pl.semaphore_wait(barrier, n_experts)
    for g in order[:-2]:
        send_group(g)

    def arrive(g):
        for p in pieces(g):
            z_copies[p].wait_recv()
        y_copies[g].start()

    def work(at):
        pre = dot(rows[at, :width], w_cat[...], 1, 0)
        gate_pre, up_pre = pre[:, :units], pre[:, units:]
        hidden_grad = dot(rows[at, width:], wd[...], 1, 1)
        sigma = 1.0 / (1.0 + jnp.exp(-gate_pre))
        activ = gate_pre * sigma
        hidden[at] = (activ * up_pre).astype(BF16)
        delta[at, :units] = (hidden_grad * up_pre * sigma * (1.0 + gate_pre * (1.0 - sigma))).astype(BF16)
        delta[at, units:] = (hidden_grad * activ).astype(BF16)
        return dot(delta[at], w_cat[...], 1, 1)

    def own_work(g):
        own_back[rows_of(g)] = work(rows_of(g))

    def mate_work(g):
        y_copies[g].wait_recv()
        mate_out[rows_of(g)] = work(rows_of(g, 1)).astype(BF16)
        b_copies[g].start()

    def give_back(g):
        b_copies[g].wait_recv()
        total = (own_back[rows_of(g)] + mate_in[rows_of(g)].astype(F32)).astype(BF16)
        ret_out[rows_of(g)] = total
        for p in range(g * per_group, (g + 1) * per_group):
            if peer_of(p) > 0:
                r_copies[p].start()
            else:
                ret_in[piece_rows(p)] = total[(p - g * per_group) * piece:(p - g * per_group + 1) * piece]

    for i in range(n_groups + 3):
        if i < n_groups:
            if order[i] == late[0]:
                sent_group(late[0])
                send_group(late[1])
            arrive(order[i])
            if i == n_groups - 3:
                send_group(late[0])
            if i == 0:
                for copy in fetch[2:]:
                    copy.wait()
            own_work(order[i])
        if 1 <= i <= n_groups:
            mate_work(order[i - 1])
        if i >= 3:
            give_back(order[i - 3])

    store = [
        pltpu.make_async_copy(src, dst, stores.at[i])
        for i, (src, dst) in enumerate(
            [(out_ref, out_hbm), (gate_ref, gate_hbm), (up_ref, up_hbm), (down_ref, down_hbm)]
        )
    ]
    tile = 256
    for at in range(0, width, tile):
        cols = pl.ds(at, tile)
        grads = dot(rows[:, cols], delta[...], 0, 0)
        gate_ref[cols] = grads[:, :units].astype(BF16)
        up_ref[cols] = grads[:, units:].astype(BF16)
    down_ref[...] = dot(hidden[...], rows[:, width:], 0, 0).astype(BF16)

    for copy in store[1:]:
        copy.start()

    for g in order:
        for p in pieces(g):
            r_copies[p].wait_recv()
    out_ref[...] = dot(spread, ret_in[...], 0, 0).astype(BF16)
    store[0].start()

    for g in range(n_groups):
        if g != late[0]:
            sent_group(g)
        for p in pieces(g):
            r_copies[p].wait_send()
        y_copies[g].wait_send()
        b_copies[g].wait_send()
    for copy in store:
        copy.wait()


def write_out(*refs):
    count = len(refs) // 2
    sems = refs[-1]
    copies = [pltpu.make_async_copy(refs[i], refs[count + i], sems.at[i]) for i in range(count)]
    for copy in copies:
        copy.start()
    for copy in copies:
        copy.wait()


def per_device(act_rows, cot_rows, expert_ids, w_gate, w_up, w_down):
    n_experts = lax.axis_size("expert")
    n_rows, width = act_rows.shape[1:]
    units = w_gate.shape[3]
    cap = 2 * n_rows // n_experts
    slots = n_experts * cap
    n_groups = slots // 32
    n_pieces = slots // min(cap, 32)
    dma = pltpu.SemaphoreType.DMA
    vmem = pl.BlockSpec(memory_space=pltpu.VMEM)
    hbm = pl.BlockSpec(memory_space=pltpu.HBM)
    shapes = (
        jax.ShapeDtypeStruct((n_rows, width), BF16),
        jax.ShapeDtypeStruct((width, units), BF16),
        jax.ShapeDtypeStruct((width, units), BF16),
        jax.ShapeDtypeStruct((units, width), BF16),
    )
    results = pl.pallas_call(
        functools.partial(kernel, n_experts, n_groups, cap),
        out_shape=shapes,
        in_specs=[hbm, hbm, vmem, hbm, hbm, hbm],
        out_specs=(hbm,) * 4,
        scratch_shapes=[
            pltpu.VMEM((n_rows, width), BF16),
            pltpu.VMEM((width, units), BF16),
            pltpu.VMEM((width, units), BF16),
            pltpu.VMEM((units, width), BF16),
            pltpu.VMEM((n_rows, width), BF16),
            pltpu.VMEM((n_rows, width), BF16),
            pltpu.VMEM((width, 2 * units), BF16),
            pltpu.VMEM((units, width), BF16),
            pltpu.VMEM((slots, 2 * width), BF16),
            pltpu.VMEM((2 * slots, 2 * width), BF16),
            pltpu.VMEM((2 * slots, 2 * units), BF16),
            pltpu.VMEM((2 * slots, units), BF16),
            pltpu.VMEM((slots, width), F32),
            pltpu.VMEM((slots, width), BF16),
            pltpu.VMEM((slots, width), BF16),
            pltpu.VMEM((slots, width), BF16),
            pltpu.VMEM((slots, width), BF16),
            dma((5,)),
            dma((4,)),
            dma((n_pieces,)),
            dma((n_pieces,)),
            dma((n_groups,)),
            dma((n_groups,)),
            dma((n_groups,)),
            dma((n_groups,)),
            dma((n_pieces,)),
            dma((n_pieces,)),
        ],
        compiler_params=pltpu.CompilerParams(
            collective_id=0, has_side_effects=True, vmem_limit_bytes=60 * 1024 * 1024
        ),
        cost_estimate=pl.CostEstimate(
            flops=32 * slots * width * units, bytes_accessed=9 * n_rows * width * 2, transcendentals=2 * slots * units
        ),
    )(act_rows[0], cot_rows[0], expert_ids.reshape(1, n_rows), w_gate[0, 0], w_up[0, 0], w_down[0, 0])
    outs = pl.pallas_call(
        write_out,
        out_shape=shapes,
        in_specs=[hbm] * 4,
        out_specs=(hbm,) * 4,
        scratch_shapes=[dma((4,))],
        cost_estimate=pl.CostEstimate(flops=0, bytes_accessed=16 * width * units, transcendentals=0),
    )(*results)
    return (outs[0][None], outs[1][None, None], outs[2][None, None], outs[3][None, None])


def solution(mesh):
    rows = P("section", "expert", None)
    weights = P("section", "expert", None, None)
    return jax.shard_map(
        per_device,
        mesh=mesh,
        in_specs=(rows, rows, rows, weights, weights, weights),
        out_specs=(rows, weights, weights, weights),
        check_vma=False,
    )
```

time: 101 us -> 156 us (1.54)
  Pallas kernels: 91 us -> 155 us
  local copies, waits for them, and re-layouts: 9.14 us -> 0 us
    pallas_call x0 -> x1, Pallas kernels: none -> 64.7 us  [per_device(): pl.pallas_call(write_out, out_shape=shapes, in_specs=[hbm] * 4, out_specs...]
    unnamed x16 -> x0, local copies, waits for them, and re-layouts: 9.02 us -> none
where the time goes in v2:
time: 156 us
  Pallas kernels  155 us (99%)
    pallas_call x1, Pallas kernels, per_device(): pl.pallas_call(functools.partial(kernel, n_experts, n_groups, cap), out_s...  90.2 us
    pallas_call x1, Pallas kernels, per_device(): pl.pallas_call(write_out, out_shape=shapes, in_specs=[hbm] * 4, out_specs...  64.7 us

profile of v2, /device:TPU:0, one launch (start us, length us, event | category | flops | bytes accessed | tf_op | source)
XLA Modules:
  0.0 155.5 jit_solution(2366919986148768718)
XLA Ops:
  0.6 90.2 %shard_map.93 = (bf16[128,2048]{1,0:T(8,128)(2,1)}, bf16[2048,128]{1,0:T(8,128)(2,1)}, bf16[2048,128]{1,0:T(8,128)(2,1)}, bf16[128,2048]{1,0:T(8,128)(2,1)}) custom-call(bf16[128,2048]{1,0:T(8,128)(2,1)} %bitcast.10, bf16[128,2048]{1,0:T(8,128)(2,1)} %bitcast.11, s32[1,128]{1,0:T(1,128)} %bitcast.19, bf16[2048,128]{1,0:T(8,128)(2,1)} %bitcast.12, ...), custom_call_target="tpu_custom_call" | custom-call | flops 2147483648 | bytes 4718592 | tf_op jit(solution)/shard_map/pallas_call | solution.py:246
  90.8 64.7 %shard_map.94 = (bf16[128,2048]{1,0:T(8,128)(2,1)}, bf16[2048,128]{1,0:T(8,128)(2,1)}, bf16[2048,128]{1,0:T(8,128)(2,1)}, bf16[128,2048]{1,0:T(8,128)(2,1)}) custom-call(bf16[128,2048]{1,0:T(8,128)(2,1)} %get-tuple-element.12.refs_0_, bf16[2048,128]{1,0:T(8,128)(2,1)} %get-tuple-element.13.refs_1_, bf16[2048,128]{1,0:T(8,128)(2,1)} %get-tuple-element.14.refs_2_, ...), custom_call_target="tpu_custom_call" | custom-call | bytes 4194304 | tf_op jit(solution)/shard_map/pallas_call | solution.py:287

commit v3 on v2

--- a/solution.py
+++ b/solution.py
@@ -128,8 +128,17 @@
             z_copies[p].wait_send()
 
     pl.semaphore_wait(barrier, n_experts)
+    held_back = order[4:6] if n_groups == 8 and n_experts == 4 else []
     for g in order[:-2]:
-        send_group(g)
+        if g not in held_back:
+            send_group(g)
+    inner = ((own + 1) // 2) % 2 == 1
+
+    if held_back:
+        @pl.when(inner)
+        def _():
+            for g in held_back:
+                send_group(g)
 
     def arrive(g):
         for p in pieces(g):
@@ -171,6 +180,11 @@
                 sent_group(late[0])
                 send_group(late[1])
             arrive(order[i])
+            if i == 3 and held_back:
+                @pl.when(jnp.logical_not(inner))
+                def _():
+                    for g in held_back:
+                        send_group(g)
             if i == n_groups - 3:
                 send_group(late[0])
             if i == 0:
@@ -216,14 +230,23 @@
         copy.wait()
 
 
-def write_out(*refs):
-    count = len(refs) // 2
-    sems = refs[-1]
-    copies = [pltpu.make_async_copy(refs[i], refs[count + i], sems.at[i]) for i in range(count)]
-    for copy in copies:
-        copy.start()
-    for copy in copies:
-        copy.wait()
+def write_out(parts, *refs):
+    ins, outs, held = refs[:4], refs[4:8], refs[8:12]
+    in_sems, out_sems = refs[12:]
+    loads, stores = [], []
+    for i in range(4):
+        size = ins[i].shape[0] // parts
+        for j in range(parts):
+            at = pl.ds(j * size, size)
+            loads.append(pltpu.make_async_copy(ins[i].at[at], held[i].at[at], in_sems.at[i, j]))
+            stores.append(pltpu.make_async_copy(held[i].at[at], outs[i].at[at], out_sems.at[i, j]))
+    for load in loads:
+        load.start()
+    for load, store in zip(loads, stores):
+        load.wait()
+        store.start()
+    for store in stores:
+        store.wait()
 
 
 def per_device(act_rows, cot_rows, expert_ids, w_gate, w_up, w_down):
@@ -285,11 +308,12 @@
         ),
     )(act_rows[0], cot_rows[0], expert_ids.reshape(1, n_rows), w_gate[0, 0], w_up[0, 0], w_down[0, 0])
     outs = pl.pallas_call(
-        write_out,
+        functools.partial(write_out, 2),
         out_shape=shapes,
         in_specs=[hbm] * 4,
         out_specs=(hbm,) * 4,
-        scratch_shapes=[dma((4,))],
+        scratch_shapes=[pltpu.VMEM(shape.shape, shape.dtype) for shape in shapes] + [dma((4, 2)), dma((4, 2))],
+        compiler_params=pltpu.CompilerParams(vmem_limit_bytes=60 * 1024 * 1024),
         cost_estimate=pl.CostEstimate(flops=0, bytes_accessed=16 * width * units, transcendentals=0),
     )(*results)
     return (outs[0][None], outs[1][None, None], outs[2][None, None], outs[3][None, None])

time: 156 us -> 93.4 us (0.60)
  Pallas kernels: 155 us -> 92.6 us
    pallas_call x1, Pallas kernels: 64.7 us -> 2.4 us  [per_device(): pl.pallas_call(functools.partial(write_out, 2), out_shape=shapes, in_spec...]
where the time goes in v3:
time: 93.4 us; the launch traced here: 93.3 us
  Pallas kernels  92.6 us (99%)
    pallas_call x1, Pallas kernels, per_device(): pl.pallas_call(functools.partial(kernel, n_experts, n_groups, cap), out_s...  90.2 us
    pallas_call x1, Pallas kernels, per_device(): pl.pallas_call(functools.partial(write_out, 2), out_shape=shapes, in_spec...  2.4 us

profile of v3, /device:TPU:0, one launch (start us, length us, event | category | flops | bytes accessed | tf_op | source)
XLA Modules:
  0.0 93.3 jit_solution(4173500635777722760)
XLA Ops:
  0.6 90.2 %shard_map.93 = (bf16[128,2048]{1,0:T(8,128)(2,1)}, bf16[2048,128]{1,0:T(8,128)(2,1)}, bf16[2048,128]{1,0:T(8,128)(2,1)}, bf16[128,2048]{1,0:T(8,128)(2,1)}) custom-call(bf16[128,2048]{1,0:T(8,128)(2,1)} %bitcast.10, bf16[128,2048]{1,0:T(8,128)(2,1)} %bitcast.11, s32[1,128]{1,0:T(1,128)} %bitcast.19, bf16[2048,128]{1,0:T(8,128)(2,1)} %bitcast.12, ...), custom_call_target="tpu_custom_call" | custom-call | flops 2147483648 | bytes 4718592 | tf_op jit(solution)/shard_map/pallas_call | solution.py:269
  90.9 2.4 %shard_map.94 = (bf16[128,2048]{1,0:T(8,128)(2,1)}, bf16[2048,128]{1,0:T(8,128)(2,1)}, bf16[2048,128]{1,0:T(8,128)(2,1)}, bf16[128,2048]{1,0:T(8,128)(2,1)}) custom-call(bf16[128,2048]{1,0:T(8,128)(2,1)} %get-tuple-element.12.refs_0_, bf16[2048,128]{1,0:T(8,128)(2,1)} %get-tuple-element.13.refs_1_, bf16[2048,128]{1,0:T(8,128)(2,1)} %get-tuple-element.14.refs_2_, ...), custom_call_target="tpu_custom_call" | custom-call | bytes 4194304 | tf_op jit(solution)/shard_map/pallas_call | solution.py:310

commit v4 on v3

--- a/solution.py
+++ b/solution.py
@@ -30,7 +30,7 @@
     n_experts, n_groups, cap,
     act_ref, cot_ref, ids_ref, wg_ref, wu_ref, wd_ref,
     out_hbm, gate_hbm, up_hbm, down_hbm,
-    out_ref, gate_ref, up_ref, down_ref, act, cot, w_cat, wd, send, rows, delta, hidden, own_back, mate_out, mate_in, ret_out, ret_in,
+    out_ref, gate_ref, up_ref, down_ref, act, cot, w_cat, wd, send, rows, delta, hidden, own_back, gate_up_sum, down_sum, mate_out, mate_in, ret_out, ret_in,
     loads, stores, zs, zr, ys, yr, bs, br, rs, rr,
 ):
     n_rows, width = act_ref.shape
@@ -145,24 +145,37 @@
             z_copies[p].wait_recv()
         y_copies[g].start()
 
-    def work(at):
-        pre = dot(rows[at, :width], w_cat[...], 1, 0)
+    def work(parts):
+        acts = jnp.concatenate([rows[at, :width] for at in parts], axis=0)
+        cots = jnp.concatenate([rows[at, width:] for at in parts], axis=0)
+        pre = dot(acts, w_cat[...], 1, 0)
         gate_pre, up_pre = pre[:, :units], pre[:, units:]
-        hidden_grad = dot(rows[at, width:], wd[...], 1, 1)
+        hidden_grad = dot(cots, wd[...], 1, 1)
         sigma = 1.0 / (1.0 + jnp.exp(-gate_pre))
         activ = gate_pre * sigma
-        hidden[at] = (activ * up_pre).astype(BF16)
-        delta[at, :units] = (hidden_grad * up_pre * sigma * (1.0 + gate_pre * (1.0 - sigma))).astype(BF16)
-        delta[at, units:] = (hidden_grad * activ).astype(BF16)
-        return dot(delta[at], w_cat[...], 1, 1)
-
-    def own_work(g):
-        own_back[rows_of(g)] = work(rows_of(g))
-
-    def mate_work(g):
-        y_copies[g].wait_recv()
-        mate_out[rows_of(g)] = work(rows_of(g, 1)).astype(BF16)
-        b_copies[g].start()
+        hid = (activ * up_pre).astype(BF16)
+        gate_delta = (hidden_grad * up_pre * sigma * (1.0 + gate_pre * (1.0 - sigma))).astype(BF16)
+        up_delta = (hidden_grad * activ).astype(BF16)
+        both = jnp.concatenate([gate_delta, up_delta], axis=1)
+        for i, at in enumerate(parts):
+            hidden[at] = hid[i * group:(i + 1) * group]
+            delta[at] = both[i * group:(i + 1) * group]
+        back = dot(both, w_cat[...], 1, 1)
+        return [back[i * group:(i + 1) * group] for i in range(len(parts))]
+
+    def joint_work(own_group, mate_group):
+        parts = []
+        if mate_group is not None:
+            y_copies[mate_group].wait_recv()
+            parts.append(rows_of(mate_group, 1))
+        if own_group is not None:
+            parts.append(rows_of(own_group))
+        back = work(parts)
+        if mate_group is not None:
+            mate_out[rows_of(mate_group)] = back[0].astype(BF16)
+            b_copies[mate_group].start()
+        if own_group is not None:
+            own_back[rows_of(own_group)] = back[-1]
 
     def give_back(g):
         b_copies[g].wait_recv()
@@ -174,42 +187,67 @@
             else:
                 ret_in[piece_rows(p)] = total[(p - g * per_group) * piece:(p - g * per_group + 1) * piece]
 
+    store = [
+        pltpu.make_async_copy(src, dst, stores.at[i])
+        for i, (src, dst) in enumerate(
+            [(out_ref, out_hbm), (gate_ref, gate_hbm), (up_ref, up_hbm), (down_ref, down_hbm)]
+        )
+    ]
+    tile = 256
+
+    def runs(groups):
+        found = []
+        for g in sorted(groups):
+            if found and found[-1][1] == g * group:
+                found[-1][1] += group
+            else:
+                found.append([g * group, (g + 1) * group])
+        return [pl.ds(part * slots + lo, hi - lo) for part in range(2) for lo, hi in found]
+
+    def summed(pick, left, right):
+        total = None
+        for at in pick:
+            term = dot(left(at), right(at), 0, 0)
+            total = term if total is None else total + term
+        return total
+
+    def early_grads():
+        pick = runs(order[:-2])
+        for at in range(0, width, tile):
+            cols = pl.ds(at, tile)
+            gate_up_sum[cols] = summed(pick, lambda r: rows[r, cols], lambda r: delta[r])
+        down_sum[...] = summed(pick, lambda r: hidden[r], lambda r: rows[r, width:])
+
+    def final_grads():
+        pick = runs(late)
+        for at in range(0, width, tile):
+            cols = pl.ds(at, tile)
+            grads = gate_up_sum[cols] + summed(pick, lambda r: rows[r, cols], lambda r: delta[r])
+            gate_ref[cols] = grads[:, :units].astype(BF16)
+            up_ref[cols] = grads[:, units:].astype(BF16)
+        down_ref[...] = (down_sum[...] + summed(pick, lambda r: hidden[r], lambda r: rows[r, width:])).astype(BF16)
+
     for i in range(n_groups + 3):
         if i < n_groups:
-            if order[i] == late[0]:
-                sent_group(late[0])
-                send_group(late[1])
             arrive(order[i])
             if i == 3 and held_back:
                 @pl.when(jnp.logical_not(inner))
                 def _():
                     for g in held_back:
                         send_group(g)
-            if i == n_groups - 3:
-                send_group(late[0])
+            if i in (n_groups - 4, n_groups - 3):
+                send_group(late[i - n_groups + 4])
             if i == 0:
                 for copy in fetch[2:]:
                     copy.wait()
-            own_work(order[i])
-        if 1 <= i <= n_groups:
-            mate_work(order[i - 1])
+        if i <= n_groups:
+            joint_work(order[i] if i < n_groups else None, order[i - 1] if i > 0 else None)
         if i >= 3:
             give_back(order[i - 3])
-
-    store = [
-        pltpu.make_async_copy(src, dst, stores.at[i])
-        for i, (src, dst) in enumerate(
-            [(out_ref, out_hbm), (gate_ref, gate_hbm), (up_ref, up_hbm), (down_ref, down_hbm)]
-        )
-    ]
-    tile = 256
-    for at in range(0, width, tile):
-        cols = pl.ds(at, tile)
-        grads = dot(rows[:, cols], delta[...], 0, 0)
-        gate_ref[cols] = grads[:, :units].astype(BF16)
-        up_ref[cols] = grads[:, units:].astype(BF16)
-    down_ref[...] = dot(hidden[...], rows[:, width:], 0, 0).astype(BF16)
-
+        if i == n_groups - 2:
+            early_grads()
+
+    final_grads()
     for copy in store[1:]:
         copy.start()
 
@@ -220,8 +258,7 @@
     store[0].start()
 
     for g in range(n_groups):
-        if g != late[0]:
-            sent_group(g)
+        sent_group(g)
         for p in pieces(g):
             r_copies[p].wait_send()
         y_copies[g].wait_send()
@@ -285,6 +322,8 @@
             pltpu.VMEM((2 * slots, 2 * units), BF16),
             pltpu.VMEM((2 * slots, units), BF16),
             pltpu.VMEM((slots, width), F32),
+            pltpu.VMEM((width, 2 * units), F32),
+            pltpu.VMEM((units, width), F32),
             pltpu.VMEM((slots, width), BF16),
             pltpu.VMEM((slots, width), BF16),
             pltpu.VMEM((slots, width), BF16),

time: 93.4 us -> 93.4 us (level)
  no operation moved by 1% of the time
where the time goes in v4:
time: 93.4 us; the launch traced here: 93.2 us
  Pallas kernels  92.6 us (99%)
    pallas_call x1, Pallas kernels, per_device(): pl.pallas_call(functools.partial(kernel, n_experts, n_groups, cap), out_s...  90.2 us
    pallas_call x1, Pallas kernels, per_device(): pl.pallas_call(functools.partial(write_out, 2), out_shape=shapes, in_spec...  2.4 us

profile of v4, /device:TPU:0, one launch (start us, length us, event | category | flops | bytes accessed | tf_op | source)
XLA Modules:
  0.0 93.2 jit_solution(2554276701985767364)
XLA Ops:
  0.6 90.2 %shard_map.93 = (bf16[128,2048]{1,0:T(8,128)(2,1)}, bf16[2048,128]{1,0:T(8,128)(2,1)}, bf16[2048,128]{1,0:T(8,128)(2,1)}, bf16[128,2048]{1,0:T(8,128)(2,1)}) custom-call(bf16[128,2048]{1,0:T(8,128)(2,1)} %bitcast.10, bf16[128,2048]{1,0:T(8,128)(2,1)} %bitcast.11, s32[1,128]{1,0:T(1,128)} %bitcast.19, bf16[2048,128]{1,0:T(8,128)(2,1)} %bitcast.12, ...), custom_call_target="tpu_custom_call" | custom-call | flops 2147483648 | bytes 4718592 | tf_op jit(solution)/shard_map/pallas_call | solution.py:306
  90.8 2.4 %shard_map.94 = (bf16[128,2048]{1,0:T(8,128)(2,1)}, bf16[2048,128]{1,0:T(8,128)(2,1)}, bf16[2048,128]{1,0:T(8,128)(2,1)}, bf16[128,2048]{1,0:T(8,128)(2,1)}) custom-call(bf16[128,2048]{1,0:T(8,128)(2,1)} %get-tuple-element.12.refs_0_, bf16[2048,128]{1,0:T(8,128)(2,1)} %get-tuple-element.13.refs_1_, bf16[2048,128]{1,0:T(8,128)(2,1)} %get-tuple-element.14.refs_2_, ...), custom_call_target="tpu_custom_call" | custom-call | bytes 4194304 | tf_op jit(solution)/shard_map/pallas_call | solution.py:349

commit v5 on v4

--- a/solution.py
+++ b/solution.py
@@ -118,6 +118,7 @@
     if n_groups == 8:
         order = [0, 1, 2, 3, 6, 7, 4, 5]
     late = order[-2:]
+    deferred = order[:2]
 
     def send_group(g):
         for p in pieces(g):
@@ -173,7 +174,8 @@
         back = work(parts)
         if mate_group is not None:
             mate_out[rows_of(mate_group)] = back[0].astype(BF16)
-            b_copies[mate_group].start()
+            if mate_group not in deferred:
+                b_copies[mate_group].start()
         if own_group is not None:
             own_back[rows_of(own_group)] = back[-1]
 
@@ -242,12 +244,17 @@
                     copy.wait()
         if i <= n_groups:
             joint_work(order[i] if i < n_groups else None, order[i - 1] if i > 0 else None)
-        if i >= 3:
+        if i == n_groups:
+            b_copies[deferred[0]].start()
+        if i >= 3 + len(deferred):
             give_back(order[i - 3])
         if i == n_groups - 2:
             early_grads()
 
+    b_copies[deferred[1]].start()
     final_grads()
+    for g in deferred:
+        give_back(g)
     for copy in store[1:]:
         copy.start()
 

time: 93.4 us -> 88.3 us (0.945)
  Pallas kernels: 92.6 us -> 87.4 us
    pallas_call x1, Pallas kernels: 90.2 us -> 85.1 us  [per_device(): pl.pallas_call(functools.partial(kernel, n_experts, n_groups, cap), out_s...]
where the time goes in v5:
time: 88.3 us; the launch traced here: 88.1 us
  Pallas kernels  87.4 us (99%)
    pallas_call x1, Pallas kernels, per_device(): pl.pallas_call(functools.partial(kernel, n_experts, n_groups, cap), out_s...  85.1 us
    pallas_call x1, Pallas kernels, per_device(): pl.pallas_call(functools.partial(write_out, 2), out_shape=shapes, in_spec...  2.4 us

profile of v5, /device:TPU:0, one launch (start us, length us, event | category | flops | bytes accessed | tf_op | source)
XLA Modules:
  0.0 88.1 jit_solution(16303193589444704270)
XLA Ops:
  0.6 85.1 %shard_map.93 = (bf16[128,2048]{1,0:T(8,128)(2,1)}, bf16[2048,128]{1,0:T(8,128)(2,1)}, bf16[2048,128]{1,0:T(8,128)(2,1)}, bf16[128,2048]{1,0:T(8,128)(2,1)}) custom-call(bf16[128,2048]{1,0:T(8,128)(2,1)} %bitcast.10, bf16[128,2048]{1,0:T(8,128)(2,1)} %bitcast.11, s32[1,128]{1,0:T(1,128)} %bitcast.19, bf16[2048,128]{1,0:T(8,128)(2,1)} %bitcast.12, ...), custom_call_target="tpu_custom_call" | custom-call | flops 2147483648 | bytes 4718592 | tf_op jit(solution)/shard_map/pallas_call | solution.py:313
  85.7 2.4 %shard_map.94 = (bf16[128,2048]{1,0:T(8,128)(2,1)}, bf16[2048,128]{1,0:T(8,128)(2,1)}, bf16[2048,128]{1,0:T(8,128)(2,1)}, bf16[128,2048]{1,0:T(8,128)(2,1)}) custom-call(bf16[128,2048]{1,0:T(8,128)(2,1)} %get-tuple-element.12.refs_0_, bf16[2048,128]{1,0:T(8,128)(2,1)} %get-tuple-element.13.refs_1_, bf16[2048,128]{1,0:T(8,128)(2,1)} %get-tuple-element.14.refs_2_, ...), custom_call_target="tpu_custom_call" | custom-call | bytes 4194304 | tf_op jit(solution)/shard_map/pallas_call | solution.py:356

commit v6 on v5

--- a/solution.py
+++ b/solution.py
@@ -109,10 +109,13 @@
 
     for i, source in enumerate((act, cot)):
         fetch[i].wait()
-        packed = dot(spread, source[...], 1, 0).astype(BF16)
-        cols = pl.ds(i * width, width)
-        send[cap:, cols] = packed[cap:]
-        rows[:cap, cols] = packed[:cap]
+        rows[:cap, pl.ds(i * width, width)] = dot(spread[:cap], source[...], 1, 0).astype(BF16)
+    pl.semaphore_wait(barrier, n_experts)
+    ready = [g for g in range(n_groups) if not pieces(g)]
+    for g in ready:
+        y_copies[g].start()
+    for i, source in enumerate((act, cot)):
+        send[cap:, pl.ds(i * width, width)] = dot(spread[cap:], source[...], 1, 0).astype(BF16)
 
     order = list(range(n_groups))
     if n_groups == 8:
@@ -128,7 +131,6 @@
         for p in pieces(g):
             z_copies[p].wait_send()
 
-    pl.semaphore_wait(barrier, n_experts)
     held_back = order[4:6] if n_groups == 8 and n_experts == 4 else []
     for g in order[:-2]:
         if g not in held_back:
@@ -144,7 +146,8 @@
     def arrive(g):
         for p in pieces(g):
             z_copies[p].wait_recv()
-        y_copies[g].start()
+        if g not in ready:
+            y_copies[g].start()
 
     def work(parts):
         acts = jnp.concatenate([rows[at, :width] for at in parts], axis=0)

time: 88.3 us -> 87.9 us (level)
  no operation moved by 1% of the time
where the time goes in v6:
time: 87.9 us; the launch traced here: 87.7 us
  Pallas kernels  87 us (99%)
    pallas_call x1, Pallas kernels, per_device(): pl.pallas_call(functools.partial(kernel, n_experts, n_groups, cap), out_s...  84.6 us
    pallas_call x1, Pallas kernels, per_device(): pl.pallas_call(functools.partial(write_out, 2), out_shape=shapes, in_spec...  2.4 us

profile of v6, /device:TPU:0, one launch (start us, length us, event | category | flops | bytes accessed | tf_op | source)
XLA Modules:
  0.0 87.7 jit_solution(17549436419122820316)
XLA Ops:
  0.6 84.6 %shard_map.93 = (bf16[128,2048]{1,0:T(8,128)(2,1)}, bf16[2048,128]{1,0:T(8,128)(2,1)}, bf16[2048,128]{1,0:T(8,128)(2,1)}, bf16[128,2048]{1,0:T(8,128)(2,1)}) custom-call(bf16[128,2048]{1,0:T(8,128)(2,1)} %bitcast.10, bf16[128,2048]{1,0:T(8,128)(2,1)} %bitcast.11, s32[1,128]{1,0:T(1,128)} %bitcast.19, bf16[2048,128]{1,0:T(8,128)(2,1)} %bitcast.12, ...), custom_call_target="tpu_custom_call" | custom-call | flops 2147483648 | bytes 4718592 | tf_op jit(solution)/shard_map/pallas_call | solution.py:316
  85.3 2.4 %shard_map.94 = (bf16[128,2048]{1,0:T(8,128)(2,1)}, bf16[2048,128]{1,0:T(8,128)(2,1)}, bf16[2048,128]{1,0:T(8,128)(2,1)}, bf16[128,2048]{1,0:T(8,128)(2,1)}) custom-call(bf16[128,2048]{1,0:T(8,128)(2,1)} %get-tuple-element.12.refs_0_, bf16[2048,128]{1,0:T(8,128)(2,1)} %get-tuple-element.13.refs_1_, bf16[2048,128]{1,0:T(8,128)(2,1)} %get-tuple-element.14.refs_2_, ...), custom_call_target="tpu_custom_call" | custom-call | bytes 4194304 | tf_op jit(solution)/shard_map/pallas_call | solution.py:359
